TPU v7x, 1024 devices: a whole 4x8x16 slice. The times are simulated.
1024 devices in a mesh: dp: 64 (over z, x_hi, core), expert: 16 (over x_lo, y).
Axes of the slice: x: 4 (x_hi: 2, x_lo: 2; x = x_hi * 2 + x_lo), y: 8, z: 16, core: 2. Of those that a mesh axis runs over, the one named last changes fastest.
Arguments:
- teacher_in: bfloat16 [8192, 2048], P('dp'), may hold values from -6 to 6
- student_in: bfloat16 [8192, 2048], P('dp'), may hold values from -6 to 6
- teacher_route: int32 [8192, 1], P('dp'), may hold values from 0 to 31, as said below
- student_route: int32 [8192, 1], P('dp'), may hold values from 0 to 31, as said below
- teacher_w1: bfloat16 [64, 2048, 2048], P('dp', None, 'expert'), may hold values from -0.125 to 0.125
- teacher_w2: bfloat16 [64, 2048, 2048], P('dp', 'expert'), may hold values from -0.09375 to 0.09375
- student_w1: bfloat16 [64, 2048, 2048], P('dp', None, 'expert'), may hold values from -0.125 to 0.125
- student_w2: bfloat16 [64, 2048, 2048], P('dp', 'expert'), may hold values from -0.09375 to 0.09375
Outputs:
- grad_w1: bfloat16 [64, 2048, 2048], P('dp', None, 'expert')
- grad_w2: bfloat16 [64, 2048, 2048], P('dp', 'expert')
Inputs may be any that keep to these rules, and one draw needn't show every extreme that they name: `teacher_route`: in each aligned block of 128 rows (the rows of one index of dp) no expert is named by more than 6 rows, and some expert exactly 6 times; every expert is named exactly 6 times in some block. `student_route`: in each aligned block of 128 rows (the rows of one index of dp) no expert is named by more than 6 rows, and some expert exactly 6 times; every expert is named exactly 6 times in some block.
All inputs are finite; a program needn't handle non-finite values.
Results may differ from a plain program's by a relative error of at most 0.015.
Values may be sent and summed in bfloat16 or wider, within the bound.
A program may use at most 64 MiB of HBM per device.

v0:
```python
import math

import jax
import jax.numpy as jnp
from jax import lax
from jax.sharding import PartitionSpec as P

root_coef = math.sqrt(2.0 / math.pi)
cubic_coef = 0.044715


def partner(value, axis, apart):
    return lax.ppermute(value, axis, [(i, i ^ 1 << apart) for i in range(lax.axis_size(axis))])


def gelu_tanh(pre_act):
    inner_arg = root_coef * (pre_act + cubic_coef * pre_act * pre_act * pre_act)
    return 0.5 * pre_act * (1.0 + jnp.tanh(inner_arg))


def gelu_slope(pre_act):
    tangent = jnp.tanh(root_coef * (pre_act + cubic_coef * pre_act * pre_act * pre_act))
    return 0.5 * (1.0 + tangent) + 0.5 * pre_act * (1.0 - tangent * tangent) * root_coef * (
        1.0 + 3.0 * cubic_coef * pre_act * pre_act
    )


def slot_table(routes, experts, capacity):
    choose = routes[:, 0]
    onehot = (choose[:, None] == jnp.arange(experts, dtype=jnp.int32)[None, :]).astype(jnp.int32)
    rank_table = jnp.cumsum(onehot, axis=0) - 1
    position = jnp.sum(onehot * rank_table, axis=1)
    slot_index = choose * capacity + position
    placing = (
        jnp.arange(experts * capacity, dtype=jnp.int32)[:, None] == slot_index[None, :]
    ).astype(jnp.bfloat16)
    return (slot_index, placing)


def place_rows(placing, row_values, experts, capacity):
    filled = jnp.dot(placing, row_values, preferred_element_type=jnp.float32).astype(jnp.bfloat16)
    return filled.reshape(experts, capacity, row_values.shape[1])


def join_halves(mine_half, other_half, half_index):
    first_half = jnp.where(half_index == 0, mine_half, other_half)
    second_half = jnp.where(half_index == 0, other_half, mine_half)
    return jnp.concatenate([first_half, second_half], axis=1)


def gather_rows(returned, slot_index, capacity):
    model_width = returned.shape[2]
    flat_rows = returned.reshape(-1, model_width)
    expert_of = slot_index // capacity
    first_row = 2 * expert_of * capacity + slot_index % capacity
    lower = jnp.take(flat_rows, first_row, axis=0).astype(jnp.float32)
    upper = jnp.take(flat_rows, first_row + capacity, axis=0).astype(jnp.float32)
    return lower + upper


def on_device(
    teacher_in,
    student_in,
    teacher_route,
    student_route,
    teacher_w1,
    teacher_w2,
    student_w1,
    student_w2,
):
    groups = lax.axis_size("dp")
    experts = groups // 2
    row_count, model_width = teacher_in.shape
    capacity = 2 * max(1, 3 * row_count // (4 * experts))
    half_index = lax.axis_index("dp") % 2
    loss_scale = 1.0 / math.sqrt(row_count)
    teacher_slot, teacher_place = slot_table(teacher_route, experts, capacity)
    student_slot, student_place = slot_table(student_route, experts, capacity)
    teacher_buffer = place_rows(teacher_place, teacher_in, experts, capacity)
    student_buffer = place_rows(student_place, student_in, experts, capacity)
    mine_teacher, mine_student = (
        lax.all_to_all(
            teacher_buffer.reshape(groups, capacity // 2, model_width),
            "dp",
            split_axis=0,
            concat_axis=0,
            tiled=True,
        ),
        lax.all_to_all(
            student_buffer.reshape(groups, capacity // 2, model_width),
            "dp",
            split_axis=0,
            concat_axis=0,
            tiled=True,
        ),
    )
    other_both = partner(jnp.stack([mine_teacher, mine_student]), "dp", 0)
    teacher_recv = join_halves(mine_teacher, other_both[0], half_index)
    student_recv = join_halves(mine_student, other_both[1], half_index)
    teacher_flat = teacher_recv.reshape(groups * capacity, model_width)
    student_flat = student_recv.reshape(groups * capacity, model_width)
    teacher_hidden = gelu_tanh(
        jnp.dot(teacher_flat, teacher_w1[0], preferred_element_type=jnp.float32)
    ).astype(jnp.bfloat16)
    teacher_part = jnp.dot(
        teacher_hidden, teacher_w2[0], preferred_element_type=jnp.float32
    ).astype(jnp.bfloat16)
    student_pre = jnp.dot(student_flat, student_w1[0], preferred_element_type=jnp.float32)
    student_hidden = gelu_tanh(student_pre).astype(jnp.bfloat16)
    student_part = jnp.dot(
        student_hidden, student_w2[0], preferred_element_type=jnp.float32
    ).astype(jnp.bfloat16)
    back_teacher, back_student = (
        lax.all_to_all(
            teacher_part.reshape(groups, capacity, model_width),
            "dp",
            split_axis=0,
            concat_axis=0,
            tiled=True,
        ),
        lax.all_to_all(
            student_part.reshape(groups, capacity, model_width),
            "dp",
            split_axis=0,
            concat_axis=0,
            tiled=True,
        ),
    )
    local_teacher = gather_rows(back_teacher, teacher_slot, capacity)
    local_student = gather_rows(back_student, student_slot, capacity)
    total_teacher, total_student = lax.psum((local_teacher, local_student), "expert")
    output_gap = total_student - total_teacher
    upstream = (output_gap * loss_scale).astype(jnp.bfloat16)
    grad_buffer = place_rows(student_place, upstream, experts, capacity)
    grad_mine = lax.all_to_all(
        grad_buffer.reshape(groups, capacity // 2, model_width),
        "dp",
        split_axis=0,
        concat_axis=0,
        tiled=True,
    )
    grad_other = partner(grad_mine, "dp", 0)
    grad_recv = join_halves(grad_mine, grad_other, half_index)
    grad_flat = grad_recv.reshape(groups * capacity, model_width)
    hidden_grad = jnp.dot(grad_flat, student_w2[0].T, preferred_element_type=jnp.float32)
    pre_grad = (hidden_grad * gelu_slope(student_pre)).astype(jnp.bfloat16)
    grad_second = jnp.dot(student_hidden.T, grad_flat, preferred_element_type=jnp.float32).astype(
        jnp.bfloat16
    )
    grad_first = jnp.dot(student_flat.T, pre_grad, preferred_element_type=jnp.float32).astype(
        jnp.bfloat16
    )
    return (grad_first[None], grad_second[None])


def solution(mesh):
    return jax.shard_map(
        on_device,
        mesh=mesh,
        in_specs=(
            P("dp", None),
            P("dp", None),
            P("dp", None),
            P("dp", None),
            P("dp", None, "expert"),
            P("dp", "expert", None),
            P("dp", None, "expert"),
            P("dp", "expert", None),
        ),
        out_specs=(P("dp", None, "expert"), P("dp", "expert", None)),
        check_vma=False,
    )
```

profile of v0, /device:TPU:1, one launch (start us, length us, event | category | flops | bytes accessed | tf_op | source)
XLA Modules:
  0.0 644.8 jit_solution(15585729064601268057)
XLA Ops:
  12.4 23.4 %all-to-all-start = ((bf16[64,3,2048]{2,1,0:T(4,128)(2,1)}), bf16[64,3,2048]{2,1,0:T(4,128)(2,1)S(1)}, u32[]{:S(2)}, u32[]{:S(2)}) async-start(bf16[64,3,2048]{2,1,0:T(4,128)(2,1)} %reshape_reshape.9), calls=%async_computation | async-start | bytes 2097152 | tf_op jit(solution)/shard_map/all_to_all | solution.py:89
  38.0 51.9 %all-to-all-done = bf16[64,3,2048]{2,1,0:T(4,128)(2,1)S(1)} async-done(((bf16[64,3,2048]{2,1,0:T(4,128)(2,1)}), bf16[64,3,2048]{2,1,0:T(4,128)(2,1)S(1)}, u32[]{:S(2)}, u32[]{:S(2)}) %all-to-all-start) | async-done | bytes 786464 | tf_op jit(solution)/shard_map/all_to_all | solution.py:89
  89.9 61.4 %all_to_all.25 = bf16[64,3,2048]{2,1,0:T(4,128)(2,1)S(1)} all-to-all(bf16[64,3,2048]{2,1,0:T(4,128)(2,1)} %reshape_reshape.10), channel_id=1, replica_groups=mesh['dp'=64,'expert'=16] {'dp'}, dimensions={0} | all-to-all | bytes 1572864 | tf_op jit(solution)/shard_map/all_to_all | solution.py:82
  151.3 1.5 pad_maximum_fusion
  152.8 2.3 copy.10
  155.1 4.4 collective-permute-start
  159.5 3.3 collective-permute-done
  164.4 4.3 broadcast_select_fusion.3
  169.8 1.5 reshape.49
  171.3 3.3 convolution_convert_fusion
  174.6 1.6 reshape.50
  176.2 5.2 all-to-all-start.3
  181.4 3.9 pad_maximum_fusion.1
  185.4 3.8 reshape.46
  189.1 2.0 fusion.9
  191.1 1.8 convolution_convert_fusion.1
  192.9 3.7 reshape.47
  196.6 83.2 %all-to-all-done.3 = bf16[64,6,2048]{2,1,0:T(8,128)(2,1)S(1)} async-done(((bf16[64,6,2048]{2,1,0:T(8,128)(2,1)}), bf16[64,6,2048]{2,1,0:T(8,128)(2,1)S(1)}, u32[]{:S(2)}, u32[]{:S(2)}) %all-to-all-start.3) | async-done | bytes 1572896 | tf_op jit(solution)/shard_map/all_to_all | solution.py:114
  281.1 8.2 %all-to-all-start.2 = ((bf16[64,6,2048]{2,1,0:T(8,128)(2,1)}), bf16[64,6,2048]{2,1,0:T(8,128)(2,1)}, u32[]{:S(2)}, u32[]{:S(2)}) async-start(bf16[64,6,2048]{2,1,0:T(8,128)(2,1)} %reshape.47), calls=%async_computation.2 | async-start | bytes 4194304 | tf_op jit(solution)/shard_map/all_to_all | solution.py:121
  289.5 2.6 reshape.51
  294.0 93.7 %all-to-all-done.2 = bf16[64,6,2048]{2,1,0:T(8,128)(2,1)} async-done(((bf16[64,6,2048]{2,1,0:T(8,128)(2,1)}), bf16[64,6,2048]{2,1,0:T(8,128)(2,1)}, u32[]{:S(2)}, u32[]{:S(2)}) %all-to-all-start.2) | async-done | bytes 1572896 | tf_op jit(solution)/shard_map/all_to_all | solution.py:121
  387.7 2.6 reshape.48
  390.3 1.7 gather_fusion
  392.1 1.7 gather_fusion.1
  396.4 141.2 %all-reduce.3.cloned.1.call-done = (f32[128,2048]{1,0:T(8,128)}, f32[128,2048]{1,0:T(8,128)}) async-done(((f32[128,2048]{1,0:T(8,128)}, f32[128,2048]{1,0:T(8,128)}), (f32[128,2048]{1,0:T(8,128)}, f32[128,2048]{1,0:T(8,128)})) %all-reduce.3.cloned.1.call-update) | async-done | bytes 2097168 | tf_op jit(solution)/shard_map/psum | solution.py:131
  537.5 1.9 convolution_convert_fusion.2
  539.9 80.6 %all_to_all.26 = bf16[64,3,2048]{2,1,0:T(4,128)(2,1)S(1)} all-to-all(bf16[64,3,2048]{2,1,0:T(4,128)(2,1)S(1)} %reshape_reshape.11), channel_id=1, replica_groups=mesh['dp'=64,'expert'=16] {'dp'}, dimensions={0} | all-to-all | bytes 1572864 | tf_op jit(solution)/shard_map/all_to_all | solution.py:135
  621.1 4.7 collective-permute-start.1
  625.8 1.7 collective-permute-done.1
  629.6 1.5 reshape.52
  631.1 2.8 fusion.1
  633.9 4.1 fusion
  (50 shorter events, 19.0 us)
Async XLA Ops:
  7.2 184.0 %copy-start = (bf16[1,128,2048]{2,1,0:T(8,128)(2,1)S(1)}, bf16[1,128,2048]{2,1,0:T(8,128)(2,1)}, u32[]{:S(2)}) copy-start(bf16[1,128,2048]{2,1,0:T(8,128)(2,1)} %param.17) | copy-start | bytes 1572868
  11.1 24.7 %copy-start.8 = (s32[128,1]{0,1:T(1,128)S(1)}, s32[128,1]{0,1:T(1,128)}, u32[]{:S(2)}) copy-start(s32[128,1]{0,1:T(1,128)} %param.12) | copy-start | bytes 1540
  12.4 23.9 %copy-start.5 = (bf16[128,2048]{1,0:T(8,128)(2,1)S(1)}, bf16[128,2048]{1,0:T(8,128)(2,1)}, u32[]{:S(2)}) copy-start(bf16[128,2048]{1,0:T(8,128)(2,1)} %param.10) | copy-start | bytes 1572868
  12.4 77.5 %all-to-all-start = ((bf16[64,3,2048]{2,1,0:T(4,128)(2,1)}), bf16[64,3,2048]{2,1,0:T(4,128)(2,1)S(1)}, u32[]{:S(2)}, u32[]{:S(2)}) async-start(bf16[64,3,2048]{2,1,0:T(4,128)(2,1)} %reshape_reshape.9), calls=%async_computation | async-start | bytes 2097152 | tf_op jit(solution)/shard_map/all_to_all | solution.py:89
  155.1 7.8 %collective-permute-start = (bf16[2,64,3,2048]{3,1,2,0:T(8,128)(2,1)}, bf16[2,64,3,2048]{3,1,2,0:T(8,128)(2,1)}, u32[]{:S(2)}, u32[]{:S(2)}) collective-permute-start(bf16[2,64,3,2048]{3,1,2,0:T(8,128)(2,1)} %copy.10), channel_id=1, source_target_pairs={{0,16},{16,0},{32,48},{48,32},{64,80},{80,64},{96,112},{112,96},{1... | collective-permute-start | bytes 4718600 | tf_op jit(solution)/shard_map/ppermute | solution.py:13
  169.8 1.5 copy-start.7
  176.2 103.6 %all-to-all-start.3 = ((bf16[64,6,2048]{2,1,0:T(8,128)(2,1)}), bf16[64,6,2048]{2,1,0:T(8,128)(2,1)S(1)}, u32[]{:S(2)}, u32[]{:S(2)}) async-start(bf16[64,6,2048]{2,1,0:T(8,128)(2,1)} %reshape.50), calls=%async_computation.3 | async-start | bytes 4194304 | tf_op jit(solution)/shard_map/all_to_all | solution.py:114
  185.4 3.8 copy-start.6
  279.8 1.3 copy-start.1
  281.1 106.6 %all-to-all-start.2 = ((bf16[64,6,2048]{2,1,0:T(8,128)(2,1)}), bf16[64,6,2048]{2,1,0:T(8,128)(2,1)}, u32[]{:S(2)}, u32[]{:S(2)}) async-start(bf16[64,6,2048]{2,1,0:T(8,128)(2,1)} %reshape.47), calls=%async_computation.2 | async-start | bytes 4194304 | tf_op jit(solution)/shard_map/all_to_all | solution.py:121
  289.4 248.2 %all-reduce.3.cloned.1.call-start = ((), (), s32[]{:S(2)}) async-start(), calls=%async_computation.5 | async-start | bytes 4194304 | tf_op jit(solution)/shard_map/psum | solution.py:131
  393.8 1.2 copy-start.3
  393.8 1.3 copy-start.4
  621.1 6.3 collective-permute-start.1
  631.1 2.8 copy-start.2
Sparse Core Ops, SparseCore 0:
  396.5 140.9 all-reduce.2
where the time goes:
time: 646 us; the launch traced here: 645 us
  waiting for transfers between devices  375 us (58%)
  blocking collectives  142 us (22%)
  starting transfers between devices  46 us (7%)
  local copies, waits for them, and re-layouts  31.5 us (5%)
  other arithmetic  18.4 us (3%)
  matrix products  17.6 us (3%)
  between operations  14.3 us (2%)
    psum x1, waiting for transfers between devices, on_device(): lax.psum((local_teacher, local_student), 'expert')  141 us
    all_to_all x1, waiting for transfers between devices, on_device(): lax.all_to_all(student_part.reshape(groups, capacity, model_width), 'dp',...  93.7 us
    all_to_all x1, waiting for transfers between devices, on_device(): lax.all_to_all(teacher_part.reshape(groups, capacity, model_width), 'dp',...  83.2 us
    all_to_all x1, blocking collectives, on_device(): lax.all_to_all(grad_buffer.reshape(groups, capacity // 2, model_width), '...  80.6 us
    all_to_all x1, blocking collectives, on_device(): lax.all_to_all(teacher_buffer.reshape(groups, capacity // 2, model_width)...  61.4 us
    all_to_all x1, waiting for transfers between devices, on_device(): lax.all_to_all(student_buffer.reshape(groups, capacity // 2, model_width)...  51.9 us
    all_to_all x1, starting transfers between devices, on_device(): lax.all_to_all(student_buffer.reshape(groups, capacity // 2, model_width)...  23.4 us
  transfers between devices with their start and end apart: 6, of which 6 were waited for; matrix products, arithmetic and copies ran while one was open for 3% of the time, Pallas kernels for 0%

commit v1 on v0

v1 whole, which is shorter than its diff:
```python
import functools
import math

import jax
import jax.numpy as jnp
from jax import lax
from jax.experimental import pallas as pl
from jax.experimental.pallas import tpu as pltpu
from jax.sharding import PartitionSpec as P

root_coef = math.sqrt(2.0 / math.pi)
cubic_coef = 0.044715
MESH = pl.DeviceIdType.MESH
F32 = jnp.float32
BF16 = jnp.bfloat16
CAP = 6
PAD = 16
X = 2


def gelu_tanh(pre_act):
    inner_arg = root_coef * (pre_act + cubic_coef * pre_act * pre_act * pre_act)
    return 0.5 * pre_act * (1.0 + jnp.tanh(inner_arg))


def gelu_slope(pre_act):
    tangent = jnp.tanh(root_coef * (pre_act + cubic_coef * pre_act * pre_act * pre_act))
    return 0.5 * (1.0 + tangent) + 0.5 * pre_act * (1.0 - tangent * tangent) * root_coef * (
        1.0 + 3.0 * cubic_coef * pre_act * pre_act
    )


def dot(a, b, ca, cb):
    return lax.dot_general(a, b, (((ca,), (cb,)), ((), ())), preferred_element_type=F32)


def iota(shape, dim):
    return lax.broadcasted_iota(jnp.int32, shape, dim)


def slot_rows(route):
    rows = route.shape[0]
    member = (route == iota((rows, 128), 1)).astype(F32)
    earlier = (iota((rows, rows), 0) >= iota((rows, rows), 1)).astype(F32)
    rank = dot(earlier.astype(BF16), member.astype(BF16), 1, 0)
    position = jnp.sum(member * rank, axis=1, keepdims=True) - 1.0
    return route * PAD + position.astype(jnp.int32)


def kernel(
    experts,
    Y,
    xt_hbm,
    xs_hbm,
    rt_ref,
    rs_ref,
    w1t_hbm,
    w2t_hbm,
    w1s_hbm,
    w2s_hbm,
    g1_ref,
    g2_ref,
    xcol,
    w1t,
    w2t,
    w1s,
    w2s,
    place,
    gapper,
    out1,
    in1,
    out2,
    in2,
    out3,
    in3,
    xt,
    xs,
    gr,
    pt,
    ps,
    lt,
    ls,
    landt,
    lands,
    staget,
    stages,
    finals,
    xsend,
    xland,
    pre_ref,
    hid_ref,
    load_sem,
    a_send,
    a_recv,
    g_send,
    g_recv,
    r_send,
    r_recv,
):
    H = Y // 2
    tokens, C = xcol.shape[1], xcol.shape[2]
    R = experts * CAP
    per = min(8, experts)
    groups = experts // per
    me = lax.axis_index("dp")
    mine = lax.axis_index("expert")
    k, c = me // 2, me % 2
    x, y = mine // Y, mine % Y
    up_y, down_y = (y + 1) % Y, (y + Y - 1) % Y

    here = (me, mine)
    sibling = (k * 2 + 1 - c, mine)
    across = (me, (1 - x) * Y + y)
    above = (me, x * Y + up_y)
    below = (me, x * Y + down_y)

    def remote(src, dst, send, recv, device):
        return pltpu.make_async_remote_copy(
            src_ref=src, dst_ref=dst, send_sem=send, recv_sem=recv, device_id=device, device_id_type=MESH
        )

    barrier = pltpu.get_barrier_semaphore()

    def greet(j, carry):
        pl.semaphore_signal(
            barrier, inc=1, device_id=(((k + j) % experts) * 2 + c, mine), device_id_type=MESH
        )
        return carry

    lax.fori_loop(1, experts, greet, 0)
    for device in (sibling, across, above, below):
        pl.semaphore_signal(barrier, inc=1, device_id=device, device_id_type=MESH)

    columns = pl.ds(pl.multiple_of(mine * C, C), C)
    loads = [
        pltpu.make_async_copy(xt_hbm.at[:, columns], xcol.at[0], load_sem.at[0]),
        pltpu.make_async_copy(xs_hbm.at[:, columns], xcol.at[1], load_sem.at[1]),
        pltpu.make_async_copy(w1t_hbm, w1t, load_sem.at[2]),
        pltpu.make_async_copy(w2t_hbm, w2t, load_sem.at[3]),
        pltpu.make_async_copy(w1s_hbm, w1s, load_sem.at[4]),
        pltpu.make_async_copy(w2s_hbm, w2s, load_sem.at[5]),
    ]
    for load in loads:
        load.start()

    lanes = iota((tokens, experts * PAD), 1)
    from_t = (slot_rows(rt_ref[...]) == lanes).astype(F32)
    from_s = (slot_rows(rs_ref[...]) + CAP == lanes).astype(F32)
    gapper[...] = (from_s - from_t).astype(BF16)
    place[0] = from_t.astype(BF16)
    place[1] = from_s.astype(BF16)

    half = per * CAP
    col = iota((2 * half, per * PAD), 1)
    block, lane = col // PAD, col % PAD
    target = jnp.where(
        lane < CAP,
        block * CAP + lane,
        jnp.where(lane < 2 * CAP, half + block * CAP + lane - CAP, -1),
    )
    pack = (iota((2 * half, per * PAD), 0) == target).astype(F32).astype(BF16)

    loads[0].wait()
    loads[1].wait()
    both = jnp.concatenate([place[0], place[1]], axis=0)
    values = jnp.concatenate([xcol[0], xcol[1]], axis=0)
    out1[...] = dot(both, values, 0, 0).astype(BF16).reshape(experts, PAD, C)

    pl.semaphore_wait(barrier, experts - 1 + 4)

    def exchange_start(n, src, dst):
        def send(j, carry):
            other = (k + j) % experts
            remote(src.at[other], dst.at[k], a_send.at[n], a_recv.at[n], (other * 2 + c, mine)).start()
            return carry

        lax.fori_loop(1, experts, send, 0)
        dst[k] = src[k]

    def exchange_wait(n, dst):
        if experts > 1:
            many = dst.at[pl.ds(0, experts - 1)]
            pltpu.make_async_copy(many, many, a_recv.at[n]).wait()

    def exchange_sent(n, src):
        if experts > 1:
            many = src.at[pl.ds(0, experts - 1)]
            pltpu.make_async_copy(many, many, a_send.at[n]).wait()

    started = []

    def go(copy):
        copy.start()
        started.append(copy)
        return copy

    lower, upper = pl.ds(0, R // 2), pl.ds(R // 2, R // 2)

    class Gather:
        def __init__(self, n, buf):
            self.n, self.buf, self.siblings = n, buf, 0
            own = buf.at[c, y, x]
            self.cross = go(remote(own, own, g_send.at[n, 0], g_recv.at[n, 0], across))
            self.ring = {}

        def to_sibling(self, part):
            i = 1 + 2 * H + self.siblings
            self.siblings += 1
            go(remote(part, part, g_send.at[self.n, i], g_recv.at[self.n, 1 + 2 * H], sibling))

        def send(self, way, s):
            from_y = (y + Y - (s - 1)) % Y if way == 0 else (y + s - 1) % Y
            part = self.buf.at[self_c, from_y]
            if s == H:
                part = part.at[:, lower if way == 0 else upper]
            i = 1 + way * H + s - 1
            self.ring[way, s] = go(
                remote(part, part, g_send.at[self.n, i], g_recv.at[self.n, i], above if way == 0 else below)
            )

        def step(self, s):
            if s == 0:
                self.cross.wait_recv()
                self.send(0, 1)
                self.send(1, 1)
                self.to_sibling(self.buf.at[c, y])
                return
            for way in (0, 1):
                self.ring[way, s].wait_recv()
                if s < H:
                    self.send(way, s + 1)
                    from_y = (y + Y - s) % Y if way == 0 else (y + s) % Y
                    self.to_sibling(self.buf.at[c, from_y])
            if s == H:
                self.to_sibling(self.buf.at[c, (y + H) % Y])

        def finish(self):
            whole = self.buf.at[1 - c]
            pltpu.make_async_copy(whole, whole, g_recv.at[self.n, 1 + 2 * H]).wait()

    self_c = c

    def pack_rows(src, first, dsts):
        for g in range(groups):
            rows = dot(pack[first:], src[pl.ds(g * per, per)].reshape(per * PAD, C), 1, 0).astype(BF16)
            for i, dst in enumerate(dsts):
                dst[c, y, x, pl.ds(g * half, half)] = rows[i * half : (i + 1) * half]

    exchange_start(0, out1, in1)
    exchange_wait(0, in1)
    pack_rows(in1, 0, (xt, xs))

    gathers = [Gather(0, xt), Gather(1, xs)]
    for s in range(H + 1):
        for gather in gathers:
            gather.step(s)

    def pair_cols(ref, i):
        return jnp.concatenate([ref[:, i, 0].reshape(2 * R, C), ref[:, i, 1].reshape(2 * R, C)], axis=1)

    def w1_rows(ref, i):
        first = pl.ds(pl.multiple_of(i * C, C), C)
        second = pl.ds(pl.multiple_of((Y + i) * C, C), C)
        return first, second

    def forward(buf, w1, w2, part, keep):
        def first(i, total):
            a, b = w1_rows(w1, i)
            return total + dot(pair_cols(buf, i), jnp.concatenate([w1[a], w1[b]], axis=0), 1, 0)

        pre = lax.fori_loop(0, Y, first, jnp.zeros((2 * R, w1.shape[1]), F32))
        hidden = gelu_tanh(pre).astype(BF16)
        if keep:
            pre_ref[...] = pre
        hid_ref[...] = hidden

        def second(i, carry):
            a, b = w1_rows(w1, i)
            out = dot(hid_ref[...], jnp.concatenate([w2[:, a], w2[:, b]], axis=1), 1, 0).astype(BF16)
            part[:, i, 0] = out[:, :C].reshape(2, R, C)
            part[:, i, 1] = out[:, C:].reshape(2, R, C)
            return carry

        lax.fori_loop(0, Y, second, 0)

    class Scatter:
        def __init__(self, n, part, land, ring, stage):
            self.n, self.part, self.land, self.ring, self.stage = n, part, land, ring, stage
            self.sib = go(remote(part.at[1 - c], land, r_send.at[n, 0], r_recv.at[n, 0], sibling))
            self.copies = {}

        def own(self, i):
            return self.part[c, i].astype(F32) + self.land[i].astype(F32)

        def send(self, way, s):
            dst, src = self.ring.at[way, s - 1], self.stage.at[way, s - 1]
            if s == 1:
                rows = lower if way == 0 else upper
                dst, src = dst.at[:, rows], src.at[:, rows]
            i = 1 + way * H + s - 1
            self.copies[way, s] = go(
                remote(src, dst, r_send.at[self.n, i], r_recv.at[self.n, i], above if way == 0 else below)
            )

        def step(self, s):
            if s == 1:
                self.sib.wait_recv()
                value = self.own((y + H) % Y).astype(BF16)
                self.stage[0, 0, :, : R // 2] = value[:, : R // 2]
                self.stage[1, 0, :, R // 2 :] = value[:, R // 2 :]
                self.send(0, 1)
                self.send(1, 1)
                return
            away = H + 1 - s
            for way in (0, 1):
                own = self.own((y + away) % Y if way == 0 else (y + Y - away) % Y)
                self.copies[way, s - 1].wait_recv()
                if s == 2:
                    if way == 0:
                        top = own[:, : R // 2] + self.ring[0, 0, :, : R // 2].astype(F32)
                        self.stage[0, 1, :, : R // 2] = top.astype(BF16)
                        self.stage[0, 1, :, R // 2 :] = own[:, R // 2 :].astype(BF16)
                    else:
                        low = own[:, R // 2 :] + self.ring[1, 0, :, R // 2 :].astype(F32)
                        self.stage[1, 1, :, : R // 2] = own[:, : R // 2].astype(BF16)
                        self.stage[1, 1, :, R // 2 :] = low.astype(BF16)
                else:
                    total = own + self.ring[way, s - 2].astype(F32)
                    self.stage[way, s - 1] = total.astype(BF16)
                self.send(way, s)

        def last(self):
            total = self.own(y)
            for way in (0, 1):
                self.copies[way, H].wait_recv()
                total = total + self.ring[way, H - 1].astype(F32)
            finals[self.n] = total
            xsend[self.n] = finals[self.n, 1 - x].astype(BF16)
            i = 1 + 2 * H
            self.cross = go(
                remote(xsend.at[self.n], xland.at[self.n], r_send.at[self.n, i], r_recv.at[self.n, i], across)
            )

        def result(self):
            self.cross.wait_recv()
            return (finals[self.n, x] + xland[self.n].astype(F32)).astype(BF16)

    gathers[0].finish()
    loads[2].wait()
    loads[3].wait()
    forward(xt, w1t, w2t, pt, False)
    scatters = [Scatter(0, pt, lt, landt, staget)]
    gathers[1].finish()
    loads[4].wait()
    loads[5].wait()
    forward(xs, w1s, w2s, ps, True)
    scatters.append(Scatter(1, ps, ls, lands, stages))
    for s in range(1, H + 1):
        for scatter in scatters:
            scatter.step(s)
    for scatter in scatters:
        scatter.last()
    sum_t = scatters[0].result()
    sum_s = scatters[1].result()
    for g in range(groups):
        rows = slice(g * half, (g + 1) * half)
        spread = dot(pack, jnp.concatenate([sum_t[rows], sum_s[rows]], axis=0), 0, 0)
        out2[pl.ds(g * per, per)] = spread.astype(BF16).reshape(per, PAD, C)
    exchange_start(1, out2, in2)
    exchange_wait(1, in2)

    gap = dot(gapper[...], in2[...].reshape(experts * PAD, C), 1, 0)
    upstream = (gap * (1.0 / math.sqrt(tokens))).astype(BF16)
    out3[...] = dot(place[1], upstream, 0, 0).astype(BF16).reshape(experts, PAD, C)
    exchange_start(2, out3, in3)
    exchange_wait(2, in3)
    pack_rows(in3, half, (gr,))
    gather = Gather(2, gr)
    for s in range(H + 1):
        gather.step(s)
    gather.finish()

    def back_hidden(i, total):
        a, b = w1_rows(w2s, i)
        cols = pair_cols(gr, i)
        second = dot(hid_ref[...], cols, 0, 0).astype(BF16)
        g2_ref[:, a] = second[:, :C]
        g2_ref[:, b] = second[:, C:]
        return total + dot(cols, jnp.concatenate([w2s[:, a], w2s[:, b]], axis=1), 1, 1)

    hidden_grad = lax.fori_loop(0, Y, back_hidden, jnp.zeros(pre_ref.shape, F32))
    pre_grad = (hidden_grad * gelu_slope(pre_ref[...])).astype(BF16)

    def back_first(i, carry):
        a, b = w1_rows(w1s, i)
        first = dot(pair_cols(xs, i), pre_grad, 0, 0).astype(BF16)
        g1_ref[a] = first[:C]
        g1_ref[b] = first[C:]
        return carry

    lax.fori_loop(0, Y, back_first, 0)

    for copy in started:
        copy.wait_send()
    for n, src in ((0, out1), (1, out2), (2, out3)):
        exchange_sent(n, src)


def on_device(teacher_in, student_in, teacher_route, student_route, w1t, w2t, w1s, w2s):
    experts = lax.axis_size("dp") // 2
    spots = lax.axis_size("expert")
    Y = spots // X
    H = Y // 2
    tokens, width = teacher_in.shape
    C = width // spots
    hid = w1t.shape[2]
    R = experts * CAP
    vmem, dma = pltpu.VMEM, pltpu.SemaphoreType.DMA
    any_spec, vmem_spec = pl.BlockSpec(memory_space=pl.ANY), pl.BlockSpec(memory_space=vmem)
    message = vmem((experts, PAD, C), BF16)
    gathered = vmem((2, Y, X, R, C), BF16)
    ring = vmem((2, H, X, R, C), BF16)
    g1, g2 = pl.pallas_call(
        functools.partial(kernel, experts, Y),
        out_shape=(
            jax.ShapeDtypeStruct((width, hid), BF16),
            jax.ShapeDtypeStruct((hid, width), BF16),
        ),
        in_specs=[any_spec, any_spec, vmem_spec, vmem_spec, any_spec, any_spec, any_spec, any_spec],
        out_specs=(vmem_spec, vmem_spec),
        scratch_shapes=[
            vmem((2, tokens, C), BF16),
            vmem((width, hid), BF16),
            vmem((hid, width), BF16),
            vmem((width, hid), BF16),
            vmem((hid, width), BF16),
            vmem((2, tokens, experts * PAD), BF16),
            vmem((tokens, experts * PAD), BF16),
            message,
            message,
            message,
            message,
            message,
            message,
            gathered,
            gathered,
            gathered,
            gathered,
            gathered,
            vmem((Y, X, R, C), BF16),
            vmem((Y, X, R, C), BF16),
            ring,
            ring,
            ring,
            ring,
            vmem((2, X, R, C), F32),
            vmem((2, R, C), BF16),
            vmem((2, R, C), BF16),
            vmem((2 * R, hid), F32),
            vmem((2 * R, hid), BF16),
            dma((6,)),
            dma((3,)),
            dma((3,)),
            dma((3, 1 + 2 * H + Y)),
            dma((3, 2 + 2 * H)),
            dma((2, 2 + 2 * H)),
            dma((2, 2 + 2 * H)),
        ],
        compiler_params=pltpu.CompilerParams(
            collective_id=0, has_side_effects=True, vmem_limit_bytes=40 * 1024 * 1024
        ),
    )(teacher_in, student_in, teacher_route, student_route, w1t[0], w2t[0], w1s[0], w2s[0])
    return g1[None], g2[None]


def solution(mesh):
    return jax.shard_map(
        on_device,
        mesh=mesh,
        in_specs=(
            P("dp", None),
            P("dp", None),
            P("dp", None),
            P("dp", None),
            P("dp", None, "expert"),
            P("dp", "expert", None),
            P("dp", None, "expert"),
            P("dp", "expert", None),
        ),
        out_specs=(P("dp", None, "expert"), P("dp", "expert", None)),
        check_vma=False,
    )
```

time: 646 us -> 143 us (0.22)
  waiting for transfers between devices: 375 us -> 0 us
  blocking collectives: 142 us -> 0 us
  Pallas kernels: 0 us -> 132 us
  starting transfers between devices: 46 us -> 0 us
  local copies, waits for them, and re-layouts: 31.5 us -> 9.25 us
  other arithmetic: 18.4 us -> 0 us
  matrix products: 17.6 us -> 0 us
  between operations: 14.3 us -> 0.66 us
    all_to_all x3 -> x0, waiting for transfers between devices: 229 us -> none  [the longest x1 93.7 us: on_device(): lax.all_to_all(student_part.reshape(groups, capacity, model_width), 'dp',...]
    all_to_all x2 -> x0, blocking collectives: 142 us -> none  [the longest x1 80.6 us: on_device(): lax.all_to_all(grad_buffer.reshape(groups, capacity // 2, model_width), '...]
    psum x1 -> x0, waiting for transfers between devices: 141 us -> none  [on_device(): lax.psum((local_teacher, local_student), 'expert')]
    pallas_call x0 -> x1, Pallas kernels: none -> 132 us  [on_device(): pl.pallas_call(functools.partial(kernel, experts, Y), out_shape=(jax.Shap...]
    all_to_all x3 -> x0, starting transfers between devices: 36.8 us -> none  [the longest x1 23.4 us: on_device(): lax.all_to_all(student_buffer.reshape(groups, capacity // 2, model_width)...]
    dot_general x8 -> x0, matrix products: 17.6 us -> none  [the longest x1 4.06 us: on_device(): jnp.dot(student_flat.T, pre_grad, preferred_element_type=jnp.float32)]
    reshape x7 -> x0, local copies, waits for them, and re-layouts: 17.2 us -> none  [the longest x2 5.21 us: gather_rows(): flat_rows = returned.reshape(-1, model_width)]
    ppermute x2 -> x0, starting transfers between devices: 9.11 us -> none  [partner(): lax.ppermute(value, axis, [(i, i ^ 1 << apart) for i in range(lax.axis_si...]
  transfers between devices with their start and end apart: 6 -> 0, of which waited for: 6 -> 0; matrix products, arithmetic and copies ran while one was open for 3% -> 0% of each run, Pallas kernels for 0% -> 0%
where the time goes in v1:
time: 143 us; the launch traced here: 142 us
  Pallas kernels  132 us (92%)
  local copies, waits for them, and re-layouts  9.25 us (6%)
    pallas_call x1, Pallas kernels, on_device(): pl.pallas_call(functools.partial(kernel, experts, Y), out_shape=(jax.Shap...  132 us
    unnamed x20, local copies, waits for them, and re-layouts  9.25 us

profile of v1, /device:TPU:1, one launch (start us, length us, event | category | flops | bytes accessed | tf_op | source)
XLA Modules:
  0.0 142.4 jit_solution(14917180571853180310)
XLA Ops:
  0.6 0.0 copy-start.6
  0.6 0.6 copy-done.6
  1.3 0.0 copy-start.7
  1.3 0.1 copy.10.rt_ref
  1.4 0.5 copy-done.7
  1.9 0.1 copy.11.rs_ref
  2.1 0.0 copy-start
  2.1 1.0 copy-done
  3.1 0.0 copy-start.1
  3.1 1.0 copy-done.1
  4.1 0.0 copy-start.2
  4.1 1.0 copy-done.2
  5.2 0.0 copy-start.3
  5.2 1.0 copy-done.3
  6.2 0.0 copy-start.4
  6.2 1.0 copy-done.4
  7.3 0.0 copy-start.5
  7.3 1.0 copy-done.5
  8.3 132.4 %shard_map.95 = (bf16[2048,128]{1,0:T(8,128)(2,1)S(1)}, bf16[128,2048]{1,0:T(8,128)(2,1)S(1)}) custom-call(bf16[128,2048]{1,0:T(8,128)(2,1)S(1)} %copy-done, bf16[128,2048]{1,0:T(8,128)(2,1)S(1)} %copy-done.1, s32[128,1]{1,0:T(8,128)S(1)} %copy.10.rt_ref, s32[128,1]{1,0:T(8,128)S(1)} %copy.11.rs_ref, bf16[2048,128]{1,0:T(8,128)(2,1)S(1)} %bitcast.6, ...), custom_call_target="tpu_custom_call" | custom-call | tf_op jit(solution)/shard_map/pallas_call | solution.py:423
  140.8 0.8 copy.14
  141.6 0.8 copy.15
Async XLA Ops:
  0.6 0.7 copy-start.6
  1.3 0.7 copy-start.7
  2.1 1.0 copy-start
  3.1 1.0 copy-start.1
  4.1 1.0 copy-start.2
  5.2 1.0 copy-start.3
  6.2 1.0 copy-start.4
  7.3 1.0 copy-start.5

commit v2 on v1

v2 whole, which is shorter than its diff:
```python
import functools
import math

import jax
import jax.numpy as jnp
from jax import lax
from jax.experimental import pallas as pl
from jax.experimental.pallas import tpu as pltpu
from jax.sharding import PartitionSpec as P

root_coef = math.sqrt(2.0 / math.pi)
cubic_coef = 0.044715
MESH = pl.DeviceIdType.MESH
F32 = jnp.float32
BF16 = jnp.bfloat16
CAP = 6
PAD = 16
X = 2


def gelu_tanh(pre_act):
    inner_arg = root_coef * (pre_act + cubic_coef * pre_act * pre_act * pre_act)
    return 0.5 * pre_act * (1.0 + jnp.tanh(inner_arg))


def gelu_slope(pre_act):
    tangent = jnp.tanh(root_coef * (pre_act + cubic_coef * pre_act * pre_act * pre_act))
    return 0.5 * (1.0 + tangent) + 0.5 * pre_act * (1.0 - tangent * tangent) * root_coef * (
        1.0 + 3.0 * cubic_coef * pre_act * pre_act
    )


def dot(a, b, ca=1, cb=0):
    return lax.dot_general(a, b, (((ca,), (cb,)), ((), ())), preferred_element_type=F32)


def iota(shape, dim):
    return lax.broadcasted_iota(jnp.int32, shape, dim)


def cat(parts, axis):
    return jnp.concatenate(parts, axis=axis)


def slot_rows(route):
    tokens = route.shape[1]
    member = (route == iota((128, tokens), 0)).astype(F32)
    earlier = (iota((tokens, tokens), 0) <= iota((tokens, tokens), 1)).astype(F32)
    rank = dot(member.astype(BF16), earlier.astype(BF16))
    position = jnp.sum(member * rank, axis=0, keepdims=True) - 1.0
    return route * PAD + position.astype(jnp.int32)


def kernel(
    experts,
    Y,
    xt_hbm,
    xs_hbm,
    rt_hbm,
    rs_hbm,
    w1t_hbm,
    w2t_hbm,
    w1s_hbm,
    w2s_hbm,
    g1_ref,
    g2_ref,
    xcol,
    routes,
    w1t,
    w2t,
    w1s,
    w2s,
    place,
    back,
    out1,
    in1,
    out2,
    in2,
    out3,
    in3,
    xt,
    xs,
    gr,
    part,
    ring,
    stage,
    finals,
    xsend,
    xland,
    ups,
    pre_ref,
    hid_ref,
    hid_own,
    hid_other,
    dpre_own,
    dpre_other,
    load_sem,
    w_send,
    w_recv,
    a_send,
    a_recv,
    g_send,
    g_recv,
    s_send,
    s_recv,
    r_send,
    r_recv,
):
    H = Y // 2
    tokens, C = xcol.shape[1], xcol.shape[2]
    R = experts * CAP
    Z = experts // 2
    many = experts // 2
    per = min(8, many)
    half = per * CAP
    G = R // 2
    me = lax.axis_index("dp")
    mine = lax.axis_index("expert")
    k, c = me // 2, me % 2
    z, far = k // 2, k % 2
    x, y = mine // Y, mine % Y

    here_x = x * Y
    sibling = (k * 2 + 1 - c, mine)
    across = (me, (1 - x) * Y + y)
    above = (me, here_x + (y + 1) % Y)
    below = (me, here_x + (y + Y - 1) % Y)

    def remote(src, dst, send, recv, device):
        return pltpu.make_async_remote_copy(
            src_ref=src, dst_ref=dst, send_sem=send, recv_sem=recv, device_id=device, device_id_type=MESH
        )

    started = []

    def go(copy):
        copy.start()
        started.append(copy)
        return copy

    barrier = pltpu.get_barrier_semaphore()

    def greet(j, carry):
        pl.semaphore_signal(
            barrier, inc=1, device_id=(((k + j) % experts) * 2 + c, mine), device_id_type=MESH
        )
        return carry

    lax.fori_loop(1, experts, greet, 0)
    for device in (sibling, across, above, below):
        pl.semaphore_signal(barrier, inc=1, device_id=device, device_id_type=MESH)

    def span(i):
        return pl.ds(pl.multiple_of(i * C, C), C), pl.ds(pl.multiple_of((Y + i) * C, C), C)

    weights = ((w1t_hbm, w1t), (w2t_hbm, w2t), (w1s_hbm, w1s), (w2s_hbm, w2s))
    loads = [
        pltpu.make_async_copy(rt_hbm, routes.at[0], load_sem.at[0]),
        pltpu.make_async_copy(rs_hbm, routes.at[1], load_sem.at[1]),
    ]
    for n, source in enumerate((xt_hbm, xs_hbm)):
        for i, columns in enumerate(span(y)):
            at = 2 * n + i
            loads.append(pltpu.make_async_copy(source.at[:, columns], xcol.at[at], load_sem.at[2 + at]))
    loads += [pltpu.make_async_copy(w, v.at[c], load_sem.at[6 + i]) for i, (w, v) in enumerate(weights)]
    for load in loads:
        load.start()

    rows = iota((experts * PAD, tokens), 0)

    def one_hot(slots):
        return (slots == rows).astype(F32)

    def to_blocks(n, a, b):
        lhs = cat([place[2 * n], place[2 * n + 1]], 1)
        return dot(lhs, cat([a, b], 0)).astype(BF16).reshape(experts, PAD, C)

    loads[0].wait()
    slot_t = slot_rows(routes[0])
    place[0] = one_hot(slot_t).astype(BF16)
    place[1] = one_hot(slot_t + CAP).astype(BF16)
    loads[2].wait()
    loads[3].wait()
    out1[0] = to_blocks(0, xcol[0], xcol[1])

    col = iota((2 * half, per * PAD), 1)
    block, lane = col // PAD, col % PAD
    target = jnp.where(
        lane < CAP,
        block * CAP + lane,
        jnp.where(lane < 2 * CAP, half + block * CAP + lane - CAP, -1),
    )
    pack = (iota((2 * half, per * PAD), 0) == target).astype(F32).astype(BF16)

    pl.semaphore_wait(barrier, experts - 1 + 4)

    def shift(r):
        i = r // 2
        odd = i % 2
        return odd * ((i + 1) // 2) + (1 - odd) * (Z - i // 2)

    def towards(r):
        return ((z + shift(r)) % Z) * 2 + (far + r) % 2

    def back_from(r):
        return ((z + 2 * Z - shift(r)) % Z) * 2 + (far + r) % 2

    def dispatch(n, src, dst):
        dst[0] = src[k]
        for g in range(2):

            def send(r, carry):
                other = towards(r)
                remote(
                    src.at[other], dst.at[r], a_send.at[n], a_recv.at[n, g], (other * 2 + c, mine)
                ).start()
                return carry

            lax.fori_loop(max(1, g * many), (g + 1) * many, send, 0)

    def wait_blocks(ref, count, sem):
        if count:
            blocks = ref.at[pl.ds(0, count)]
            pltpu.make_async_copy(blocks, blocks, sem).wait()

    def dispatch_wait(n, dst, g):
        wait_blocks(dst, many if g else many - 1, a_recv.at[n, g])

    def give_back(g):
        def send(r, carry):
            other = back_from(r)
            remote(
                out2.at[r], in2.at[k], a_send.at[3], a_recv.at[3, 0], (other * 2 + c, mine)
            ).start()
            return carry

        lax.fori_loop(max(1, g * many), (g + 1) * many, send, 0)
        if g == 0:
            in2[k] = out2[0]

    def group_rows(g):
        return pl.ds(g * G, G)

    def split_rows(g, way):
        return pl.ds(g * G + way * (G // 2), G // 2)

    class Gather:
        def __init__(self, n, buf, g):
            self.n, self.buf, self.g = n, buf, g
            self.ring = {}

        def send(self, way, s):
            from_y = (y + Y - (s - 1)) % Y if way == 0 else (y + s - 1) % Y
            rows = group_rows(self.g) if s < H else split_rows(self.g, way)
            chunk = self.buf.at[from_y, :, rows]
            i = way * H + s - 1
            self.ring[way, s] = go(
                remote(chunk, chunk, g_send.at[self.n, i], g_recv.at[self.n, i], above if way == 0 else below)
            )

        def step(self, s):
            if s == 0:
                self.send(0, 1)
                self.send(1, 1)
                return
            for way in (0, 1):
                self.ring[way, s].wait_recv()
                if s < H:
                    self.send(way, s + 1)

    def arrived(s):
        if s == 0:
            return [y]
        if s == H:
            return [(y + H) % Y]
        return [(y + Y - s) % Y, (y + s) % Y]

    def pack_rows(src, g):
        for b in range(many // per):
            blocks = src[pl.ds(g * many + b * per, per)].reshape(per * PAD, C)
            packed = dot(pack, blocks)
            yield pl.ds(g * G + b * half, half), packed[:half], packed[half:]

    def unpack_in(src, g, dst):
        for rows, first, second in pack_rows(src, g):
            dst[y, 0, rows] = first.astype(BF16)
            dst[y, 1, rows] = second.astype(BF16)

    def w1_rows(w, i):
        a, b = span(i)
        return cat([cat([w[0, a], w[1, a]], 1), cat([w[0, b], w[1, b]], 1)], 0)

    def w2_cols(w, i):
        a, b = span(i)
        return cat([cat([w[0, :, a], w[0, :, b]], 1), cat([w[1, :, a], w[1, :, b]], 1)], 0)

    def pair(buf, i):
        return cat([buf[i, 0], buf[i, 1]], 1)

    def add_pre(n, s):
        buf, w = ((xt, w1t), (xs.at[c], w1s))[n]
        total = pre_ref[n] if s else None
        for i in arrived(s):
            product = dot(pair(buf, i), w1_rows(w, i))
            total = product if total is None else total + product
        pre_ref[n] = total

    dispatch(0, out1.at[0], in1.at[0])
    swaps = [go(remote(w, v.at[c], w_send.at[i], w_recv.at[i], sibling)) for i, (w, v) in enumerate(weights)]
    loads[1].wait()
    slot_s = slot_rows(routes[1])
    place[2] = one_hot(slot_s).astype(BF16)
    place[3] = one_hot(slot_s + CAP).astype(BF16)
    loads[4].wait()
    loads[5].wait()
    out1[1] = to_blocks(1, xcol[2], xcol[3])
    dispatch(1, out1.at[1], in1.at[1])
    back[0] = jnp.transpose(one_hot(slot_t)).astype(BF16)
    back[1] = jnp.transpose(one_hot(slot_t + CAP)).astype(BF16)

    gather_t = [Gather(g, xt, g) for g in range(2)]
    for g in range(2):
        dispatch_wait(0, in1.at[0], g)
        unpack_in(in1.at[0], g, xt)
        gather_t[g].step(0)
    loads[6].wait()
    swaps[0].wait_recv()
    add_pre(0, 0)
    for s in range(1, H):
        gather_t[0].step(s)
        gather_t[1].step(s)
        add_pre(0, s)
    gather_t[0].step(H)
    gather_t[1].step(H)

    def slot(d):
        return 0 if d == H else 2 * (H - abs(d)) - (1 if d > 0 else 0) if d else 2 * H - 1

    def make_part(n, d):
        i = (y + Y + d) % Y
        out = dot(hid_ref[n], w2_cols((w2t, w2s)[n], i))
        part[n, slot(d), 0] = out[:, :C]
        part[n, slot(d), 1] = out[:, C:]

    class Scatter:
        def __init__(self, n, g):
            self.n, self.g, self.m = n, g, 2 * n + g
            self.copies = {}

        def send(self, way, s):
            rows = group_rows(self.g) if s > 1 else split_rows(self.g, way)
            src, dst = stage.at[self.n, way, s - 1, :, rows], ring.at[self.n, way, s - 1, :, rows]
            i = way * H + s - 1
            self.copies[way, s] = go(
                remote(src, dst, r_send.at[self.m, i], r_recv.at[self.m, i], above if way == 0 else below)
            )

        def step(self, s):
            n = self.n
            if s == 1:
                rows = group_rows(self.g)
                stage[n, 0, 0, :, rows] = part[n, 0, :, rows].astype(BF16)
                stage[n, 1, 0, :, rows] = part[n, 0, :, rows].astype(BF16)
                self.send(0, 1)
                self.send(1, 1)
                return
            d = H + 1 - s
            for way in (0, 1):
                at = slot(d if way == 0 else -d)
                self.copies[way, s - 1].wait_recv()
                for w in (0, 1):
                    rows = split_rows(self.g, w)
                    total = part[n, at, :, rows]
                    if s > 2 or w == way:
                        total = total + ring[n, way, s - 2, :, rows].astype(F32)
                    stage[n, way, s - 1, :, rows] = total.astype(BF16)
                self.send(way, s)

        def last(self):
            n, rows = self.n, group_rows(self.g)
            total = part[n, slot(0), :, rows]
            for way in (0, 1):
                self.copies[way, H].wait_recv()
                total = total + ring[n, way, H - 1, :, rows].astype(F32)
            return total

    def far_parts(n, s):
        for d in (H + 1 - s, s - H - 1):
            make_part(n, d)

    def scatter_step(n, s):
        for g in (1, 0):
            scatters[n][g].step(s)

    scatters = [[Scatter(n, g) for g in range(2)] for n in (0, 1)]
    gather_s = [Gather(2 + g, xs.at[c], g) for g in range(2)]

    add_pre(0, H)
    hid_ref[0] = gelu_tanh(pre_ref[0]).astype(BF16)
    loads[7].wait()
    swaps[1].wait_recv()
    make_part(0, H)
    scatter_step(0, 1)
    for g in range(2):
        dispatch_wait(1, in1.at[1], g)
        unpack_in(in1.at[1], g, xs.at[c])
        gather_s[g].step(0)
    loads[8].wait()
    swaps[2].wait_recv()
    for s in range(2, H + 1):
        far_parts(0, s)
        scatter_step(0, s)
        gather_s[0].step(s - 1)
        gather_s[1].step(s - 1)
        add_pre(1, s - 2)
    make_part(0, 0)
    for g in (1, 0):
        total = scatters[0][g].last().astype(BF16)
        for b in range(many // per):
            rows_b = slice(b * half, (b + 1) * half)
            spread = dot(pack, cat([total[0, rows_b], total[1, rows_b]], 0), 0, 0)
            out2[pl.ds(g * many + b * per, per)] = spread.astype(BF16).reshape(per, PAD, C)
        give_back(g)

    gather_s[0].step(H)
    gather_s[1].step(H)
    add_pre(1, H - 1)
    add_pre(1, H)
    hid_ref[1] = gelu_tanh(pre_ref[1]).astype(BF16)
    loads[9].wait()
    swaps[3].wait_recv()
    make_part(1, H)
    scatter_step(1, 1)
    hid_own[0] = hid_ref[1, :, :C]
    hid_own[1] = hid_ref[1, :, C:]
    hid_swap = go(remote(hid_own.at[1 - c], hid_other, s_send.at[0], s_recv.at[0], sibling))
    xs_swap = go(remote(xs.at[c], xs.at[c], s_send.at[1], s_recv.at[1], sibling))
    far_parts(1, 2)
    scatter_step(1, 2)
    for s in range(3, H + 1):
        far_parts(1, s)
    make_part(1, 0)

    wait_blocks(in2, experts - 1, a_recv.at[3, 0])
    came = in2[...].reshape(experts * PAD, C)
    mine_t = [dot(back[i], came) for i in (0, 1)]
    for i in (0, 1):
        ups[0, i] = mine_t[i].astype(BF16)
    up_swap = go(remote(ups.at[0], ups.at[1], s_send.at[2], s_recv.at[2], across))
    for s in range(3, H):
        scatter_step(1, s)
    up_swap.wait_recv()
    full_t = [(mine_t[i] + ups[1, i].astype(F32)).astype(BF16) for i in (0, 1)]
    out3[...] = to_blocks(1, full_t[0], full_t[1])
    dispatch(2, out3, in3)
    if H > 2:
        scatter_step(1, H)
    x_swaps = []
    for g in (1, 0):
        total = scatters[1][g].last()
        finals[:, group_rows(g)] = total
        xsend[:, group_rows(g)] = total.astype(BF16)
        x_swaps.append(
            go(
                remote(
                    xsend.at[:, group_rows(g)],
                    xland.at[:, group_rows(g)],
                    s_send.at[5 + g],
                    s_recv.at[5 + g],
                    across,
                )
            )
        )
    for copy in x_swaps:
        copy.wait_recv()

    sib_sent = [0]

    def to_sibling(i, rows):
        chunk = gr.at[c, i, :, rows]
        at = 7 + sib_sent[0]
        sib_sent[0] += 1
        go(remote(chunk, chunk, s_send.at[at], s_recv.at[3], sibling))

    gather_g = [Gather(4 + g, gr.at[c], g) for g in range(2)]

    def grad_step(g, s):
        gather_g[g].step(s)
        for i in arrived(s):
            to_sibling(i, group_rows(g))

    def add_hidden_grad(i, total):
        product = dot(pair(gr.at[c], i), w2_cols(w2s, i), 1, 1)
        return product if total is None else total + product

    scale = 1.0 / math.sqrt(tokens)
    for g in range(2):
        dispatch_wait(2, in3, g)
        for rows_b, first, second in pack_rows(in3, g):
            for i, value in ((0, first), (1, second)):
                student = finals[i, rows_b] + xland[i, rows_b].astype(F32)
                gr[c, y, i, rows_b] = ((student - value) * scale).astype(BF16)
        grad_step(g, 0)
    hidden_grad = add_hidden_grad(y, None)
    for s in range(1, H + 1):
        grad_step(0, s)
        grad_step(1, s)
        for i in arrived(s):
            hidden_grad = add_hidden_grad(i, hidden_grad)
    pre_grad = (hidden_grad * gelu_slope(pre_ref[1])).astype(BF16)
    dpre_own[0] = pre_grad[:, :C]
    dpre_own[1] = pre_grad[:, C:]
    dpre_swap = go(remote(dpre_own.at[1 - c], dpre_other, s_send.at[3], s_recv.at[4], sibling))

    hid_swap.wait_recv()
    whole = gr.at[1 - c]
    pltpu.make_async_copy(whole, whole, s_recv.at[3]).wait()
    hidden_all = cat([hid_own[c], hid_other[...]], 0)

    def back_second(i, carry):
        a, b = span(i)
        out = dot(hidden_all, cat([pair(gr.at[c], i), pair(gr.at[1 - c], i)], 0), 0, 0).astype(BF16)
        g2_ref[:, a] = out[:, :C]
        g2_ref[:, b] = out[:, C:]
        return carry

    lax.fori_loop(0, Y, back_second, 0)
    xs_swap.wait_recv()
    dpre_swap.wait_recv()
    pre_grad_all = cat([dpre_own[c], dpre_other[...]], 0)

    def back_first(i, carry):
        a, b = span(i)
        out = dot(cat([pair(xs.at[c], i), pair(xs.at[1 - c], i)], 0), pre_grad_all, 0, 0).astype(BF16)
        g1_ref[a] = out[:C]
        g1_ref[b] = out[C:]
        return carry

    lax.fori_loop(0, Y, back_first, 0)

    for copy in started:
        copy.wait_send()
    for n, src in ((0, out1.at[0]), (1, out1.at[1]), (2, out3), (3, out2)):
        wait_blocks(src, experts - 1, a_send.at[n])


def on_device(teacher_in, student_in, teacher_route, student_route, w1t, w2t, w1s, w2s):
    experts = lax.axis_size("dp") // 2
    spots = lax.axis_size("expert")
    Y = spots // X
    H = Y // 2
    tokens, width = teacher_in.shape
    C = width // spots
    hid = w1t.shape[2]
    R = experts * CAP
    vmem, dma = pltpu.VMEM, pltpu.SemaphoreType.DMA
    hbm_spec, vmem_spec = pl.BlockSpec(memory_space=pltpu.HBM), pl.BlockSpec(memory_space=vmem)
    message = vmem((experts, PAD, C), BF16)
    around = vmem((2, 2, H, X, R, C), BF16)
    g1, g2 = pl.pallas_call(
        functools.partial(kernel, experts, Y),
        out_shape=(
            jax.ShapeDtypeStruct((width, hid), BF16),
            jax.ShapeDtypeStruct((hid, width), BF16),
        ),
        in_specs=[hbm_spec] * 8,
        out_specs=(vmem_spec, vmem_spec),
        scratch_shapes=[
            vmem((4, tokens, C), BF16),
            vmem((2, 1, tokens), jnp.int32),
            vmem((2, width, hid), BF16),
            vmem((2, hid, width), BF16),
            vmem((2, width, hid), BF16),
            vmem((2, hid, width), BF16),
            vmem((4, experts * PAD, tokens), BF16),
            vmem((2, tokens, experts * PAD), BF16),
            vmem((2, experts, PAD, C), BF16),
            vmem((2, experts, PAD, C), BF16),
            message,
            message,
            message,
            message,
            vmem((Y, X, R, C), BF16),
            vmem((2, Y, X, R, C), BF16),
            vmem((2, Y, X, R, C), BF16),
            vmem((2, Y, X, R, C), F32),
            around,
            around,
            vmem((X, R, C), F32),
            vmem((X, R, C), BF16),
            vmem((X, R, C), BF16),
            vmem((2, X, tokens, C), BF16),
            vmem((2, R, 2 * hid), F32),
            vmem((2, R, 2 * hid), BF16),
            vmem((2, R, hid), BF16),
            vmem((R, hid), BF16),
            vmem((2, R, hid), BF16),
            vmem((R, hid), BF16),
            dma((10,)),
            dma((4,)),
            dma((4,)),
            dma((4,)),
            dma((4, 2)),
            dma((6, 2 * H)),
            dma((6, 2 * H)),
            dma((7 + 2 * Y,)),
            dma((7,)),
            dma((4, 2 * H)),
            dma((4, 2 * H)),
        ],
        compiler_params=pltpu.CompilerParams(
            collective_id=0, has_side_effects=True, vmem_limit_bytes=63 * 1024 * 1024
        ),
    )(
        teacher_in,
        student_in,
        teacher_route.reshape(1, tokens),
        student_route.reshape(1, tokens),
        w1t[0],
        w2t[0],
        w1s[0],
        w2s[0],
    )
    return g1[None], g2[None]


def solution(mesh):
    return jax.shard_map(
        on_device,
        mesh=mesh,
        in_specs=(
            P("dp", None),
            P("dp", None),
            P("dp", None),
            P("dp", None),
            P("dp", None, "expert"),
            P("dp", "expert", None),
            P("dp", None, "expert"),
            P("dp", "expert", None),
        ),
        out_specs=(P("dp", None, "expert"), P("dp", "expert", None)),
        check_vma=False,
    )
```

time: 143 us -> 116 us (0.81)
  Pallas kernels: 132 us -> 112 us
  local copies, waits for them, and re-layouts: 9.25 us -> 2.72 us
    pallas_call x1, Pallas kernels: 132 us -> 112 us  [on_device(): pl.pallas_call(functools.partial(kernel, experts, Y), out_shape=(jax.Shap...]
    unnamed x20 -> x4, local copies, waits for them, and re-layouts: 9.25 us -> 2.72 us
where the time goes in v2:
time: 116 us; the launch traced here: 115 us
  Pallas kernels  112 us (97%)
  local copies, waits for them, and re-layouts  2.72 us (2%)
    pallas_call x1, Pallas kernels, on_device(): pl.pallas_call(functools.partial(kernel, experts, Y), out_shape=(jax.Shap...  112 us
    unnamed x4, local copies, waits for them, and re-layouts  2.72 us

profile of v2, /device:TPU:1, one launch (start us, length us, event | category | flops | bytes accessed | tf_op | source)
XLA Modules:
  0.0 115.5 jit_solution(11042235336283062841)
XLA Ops:
  0.6 112.1 %shard_map.95 = (bf16[2048,128]{1,0:T(8,128)(2,1)}, bf16[128,2048]{1,0:T(8,128)(2,1)}) custom-call(bf16[128,2048]{1,0:T(8,128)(2,1)} %xt_hbm.1, bf16[128,2048]{1,0:T(8,128)(2,1)} %xs_hbm.1, s32[1,128]{1,0:T(1,128)} %bitcast.14, s32[1,128]{1,0:T(1,128)} %bitcast.15, bf16[2048,128]{1,0:T(8,128)(2,1)} %bitcast.10, bf16[128,2048]{1,0:T(8,128)(2,1)} %bitcast.11, ...), custom_call_target="tpu_custom_call" | custom-call | tf_op jit(solution)/shard_map/pallas_call | solution.py:560
  112.7 0.0 copy-start
  112.7 1.9 %copy.12 = bf16[1,2048,128]{2,1,0:T(8,128)(2,1)} copy(bf16[1,2048,128]{2,1,0:T(8,128)(2,1)} %bitcast.9) | data formatting | bytes 1048576
  114.7 0.0 copy-done
  114.7 0.8 copy.13
Async XLA Ops:
  112.7 1.9 %copy-start = (bf16[128,2048]{1,0:T(8,128)(2,1)S(1)}, bf16[128,2048]{1,0:T(8,128)(2,1)}, u32[]{:S(2)}) copy-start(bf16[128,2048]{1,0:T(8,128)(2,1)} %get-tuple-element.5) | copy-start | bytes 1572868

commit v3 on v2

--- a/solution.py
+++ b/solution.py
@@ -94,6 +94,8 @@
     hid_other,
     dpre_own,
     dpre_other,
+    hid_turned,
+    xs_turned,
     load_sem,
     w_send,
     w_recv,
@@ -125,6 +127,8 @@
     across = (me, (1 - x) * Y + y)
     above = (me, here_x + (y + 1) % Y)
     below = (me, here_x + (y + Y - 1) % Y)
+    above2 = (me, here_x + (y + 2) % Y)
+    below2 = (me, here_x + (y + Y - 2) % Y)
 
     def remote(src, dst, send, recv, device):
         return pltpu.make_async_remote_copy(
@@ -147,7 +151,7 @@
         return carry
 
     lax.fori_loop(1, experts, greet, 0)
-    for device in (sibling, across, above, below):
+    for device in (sibling, across, above, below, above2, below2):
         pl.semaphore_signal(barrier, inc=1, device_id=device, device_id_type=MESH)
 
     def span(i):
@@ -192,7 +196,7 @@
     )
     pack = (iota((2 * half, per * PAD), 0) == target).astype(F32).astype(BF16)
 
-    pl.semaphore_wait(barrier, experts - 1 + 4)
+    pl.semaphore_wait(barrier, experts - 1 + 6)
 
     def shift(r):
         i = r // 2
@@ -207,16 +211,17 @@
 
     def dispatch(n, src, dst):
         dst[0] = src[k]
-        for g in range(2):
-
-            def send(r, carry):
+        for g in (1, 0):
+
+            def send(j, carry):
+                r = (g + 1) * many - 1 - j
                 other = towards(r)
                 remote(
                     src.at[other], dst.at[r], a_send.at[n], a_recv.at[n, g], (other * 2 + c, mine)
                 ).start()
                 return carry
 
-            lax.fori_loop(max(1, g * many), (g + 1) * many, send, 0)
+            lax.fori_loop(0, many if g else many - 1, send, 0)
 
     def wait_blocks(ref, count, sem):
         if count:
@@ -227,14 +232,15 @@
         wait_blocks(dst, many if g else many - 1, a_recv.at[n, g])
 
     def give_back(g):
-        def send(r, carry):
+        def send(j, carry):
+            r = (g + 1) * many - 1 - j
             other = back_from(r)
             remote(
                 out2.at[r], in2.at[k], a_send.at[3], a_recv.at[3, 0], (other * 2 + c, mine)
             ).start()
             return carry
 
-        lax.fori_loop(max(1, g * many), (g + 1) * many, send, 0)
+        lax.fori_loop(0, many if g else many - 1, send, 0)
         if g == 0:
             in2[k] = out2[0]
 
@@ -249,24 +255,20 @@
             self.n, self.buf, self.g = n, buf, g
             self.ring = {}
 
-        def send(self, way, s):
-            from_y = (y + Y - (s - 1)) % Y if way == 0 else (y + s - 1) % Y
-            rows = group_rows(self.g) if s < H else split_rows(self.g, way)
+        def send(self, way, s, to, rows, device):
+            from_y = (y + Y - s) % Y if way == 0 else (y + s) % Y
             chunk = self.buf.at[from_y, :, rows]
-            i = way * H + s - 1
-            self.ring[way, s] = go(
-                remote(chunk, chunk, g_send.at[self.n, i], g_recv.at[self.n, i], above if way == 0 else below)
-            )
+            i = way * H + to - 1
+            self.ring[way, to] = go(remote(chunk, chunk, g_send.at[self.n, i], g_recv.at[self.n, i], device))
 
         def step(self, s):
-            if s == 0:
-                self.send(0, 1)
-                self.send(1, 1)
-                return
             for way in (0, 1):
-                self.ring[way, s].wait_recv()
-                if s < H:
-                    self.send(way, s + 1)
+                if s:
+                    self.ring[way, s].wait_recv()
+                if s < H - 1:
+                    self.send(way, s, s + 1, group_rows(self.g), (above, below)[way])
+                if s == H - 2:
+                    self.send(way, s, H, split_rows(self.g, way), (above2, below2)[way])
 
     def arrived(s):
         if s == 0:
@@ -332,6 +334,7 @@
         add_pre(0, s)
     gather_t[0].step(H)
     gather_t[1].step(H)
+    add_pre(0, H)
 
     def slot(d):
         return 0 if d == H else 2 * (H - abs(d)) - (1 if d > 0 else 0) if d else 2 * H - 1
@@ -347,67 +350,74 @@
             self.n, self.g, self.m = n, g, 2 * n + g
             self.copies = {}
 
-        def send(self, way, s):
-            rows = group_rows(self.g) if s > 1 else split_rows(self.g, way)
-            src, dst = stage.at[self.n, way, s - 1, :, rows], ring.at[self.n, way, s - 1, :, rows]
-            i = way * H + s - 1
-            self.copies[way, s] = go(
-                remote(src, dst, r_send.at[self.m, i], r_recv.at[self.m, i], above if way == 0 else below)
-            )
-
-        def step(self, s):
-            n = self.n
-            if s == 1:
-                rows = group_rows(self.g)
-                stage[n, 0, 0, :, rows] = part[n, 0, :, rows].astype(BF16)
-                stage[n, 1, 0, :, rows] = part[n, 0, :, rows].astype(BF16)
-                self.send(0, 1)
-                self.send(1, 1)
-                return
-            d = H + 1 - s
+        def send(self, way, i, rows, device):
+            src, dst = stage.at[self.n, way, i, :, rows], ring.at[self.n, way, i, :, rows]
+            at = way * H + i
+            self.copies[way, i] = go(remote(src, dst, r_send.at[self.m, at], r_recv.at[self.m, at], device))
+
+        def halves(self):
             for way in (0, 1):
-                at = slot(d if way == 0 else -d)
-                self.copies[way, s - 1].wait_recv()
-                for w in (0, 1):
-                    rows = split_rows(self.g, w)
-                    total = part[n, at, :, rows]
-                    if s > 2 or w == way:
-                        total = total + ring[n, way, s - 2, :, rows].astype(F32)
-                    stage[n, way, s - 1, :, rows] = total.astype(BF16)
-                self.send(way, s)
+                rows = split_rows(self.g, way)
+                stage[self.n, way, H - 1, :, rows] = part[self.n, slot(H), :, rows].astype(BF16)
+                self.send(way, H - 1, rows, (above2, below2)[way])
+
+        def step(self, s, way):
+            n, d = self.n, H - s
+            at = slot(d if way == 0 else -d)
+            if s > 1:
+                self.copies[way, s - 2].wait_recv()
+            if s == 2:
+                self.copies[way, H - 1].wait_recv()
+            for w in (0, 1):
+                rows = split_rows(self.g, w)
+                total = part[n, at, :, rows]
+                if s > 1:
+                    total = total + ring[n, way, s - 2, :, rows].astype(F32)
+                if s == 2 and w == way:
+                    total = total + ring[n, way, H - 1, :, rows].astype(F32)
+                stage[n, way, s - 1, :, rows] = total.astype(BF16)
+            self.send(way, s - 1, group_rows(self.g), (above, below)[way])
 
         def last(self):
             n, rows = self.n, group_rows(self.g)
             total = part[n, slot(0), :, rows]
             for way in (0, 1):
-                self.copies[way, H].wait_recv()
-                total = total + ring[n, way, H - 1, :, rows].astype(F32)
+                self.copies[way, H - 2].wait_recv()
+                total = total + ring[n, way, H - 2, :, rows].astype(F32)
             return total
 
     def far_parts(n, s):
-        for d in (H + 1 - s, s - H - 1):
+        for d in (H - s, s - H):
             make_part(n, d)
 
     def scatter_step(n, s):
         for g in (1, 0):
-            scatters[n][g].step(s)
+            for way in (0, 1):
+                scatters[n][g].step(s, way)
+
+    def scatter_start(n):
+        for way in (0, 1):
+            make_part(n, (1 - 2 * way) * (H - 1))
+            for g in (1, 0):
+                scatters[n][g].step(1, way)
+        make_part(n, H)
+        for g in (1, 0):
+            scatters[n][g].halves()
 
     scatters = [[Scatter(n, g) for g in range(2)] for n in (0, 1)]
     gather_s = [Gather(2 + g, xs.at[c], g) for g in range(2)]
 
-    add_pre(0, H)
     hid_ref[0] = gelu_tanh(pre_ref[0]).astype(BF16)
     loads[7].wait()
     swaps[1].wait_recv()
-    make_part(0, H)
-    scatter_step(0, 1)
+    scatter_start(0)
     for g in range(2):
         dispatch_wait(1, in1.at[1], g)
         unpack_in(in1.at[1], g, xs.at[c])
         gather_s[g].step(0)
     loads[8].wait()
     swaps[2].wait_recv()
-    for s in range(2, H + 1):
+    for s in range(2, H):
         far_parts(0, s)
         scatter_step(0, s)
         gather_s[0].step(s - 1)
@@ -422,22 +432,21 @@
             out2[pl.ds(g * many + b * per, per)] = spread.astype(BF16).reshape(per, PAD, C)
         give_back(g)
 
-    gather_s[0].step(H)
-    gather_s[1].step(H)
+    for s in (H - 1, H):
+        gather_s[0].step(s)
+        gather_s[1].step(s)
+    add_pre(1, H - 2)
     add_pre(1, H - 1)
     add_pre(1, H)
     hid_ref[1] = gelu_tanh(pre_ref[1]).astype(BF16)
     loads[9].wait()
     swaps[3].wait_recv()
-    make_part(1, H)
-    scatter_step(1, 1)
+    scatter_start(1)
     hid_own[0] = hid_ref[1, :, :C]
     hid_own[1] = hid_ref[1, :, C:]
     hid_swap = go(remote(hid_own.at[1 - c], hid_other, s_send.at[0], s_recv.at[0], sibling))
     xs_swap = go(remote(xs.at[c], xs.at[c], s_send.at[1], s_recv.at[1], sibling))
-    far_parts(1, 2)
-    scatter_step(1, 2)
-    for s in range(3, H + 1):
+    for s in range(2, H):
         far_parts(1, s)
     make_part(1, 0)
 
@@ -447,14 +456,13 @@
     for i in (0, 1):
         ups[0, i] = mine_t[i].astype(BF16)
     up_swap = go(remote(ups.at[0], ups.at[1], s_send.at[2], s_recv.at[2], across))
-    for s in range(3, H):
-        scatter_step(1, s)
+    scatter_step(1, 2)
     up_swap.wait_recv()
     full_t = [(mine_t[i] + ups[1, i].astype(F32)).astype(BF16) for i in (0, 1)]
     out3[...] = to_blocks(1, full_t[0], full_t[1])
     dispatch(2, out3, in3)
-    if H > 2:
-        scatter_step(1, H)
+    for s in range(3, H):
+        scatter_step(1, s)
     x_swaps = []
     for g in (1, 0):
         total = scatters[1][g].last()
@@ -471,6 +479,17 @@
                 )
             )
         )
+
+    hid_swap.wait_recv()
+    hid_turned[...] = jnp.transpose(cat([hid_own[c], hid_other[...]], 0).astype(F32)).astype(BF16)
+    xs_swap.wait_recv()
+
+    def turn(i, carry):
+        rows_i = cat([pair(xs.at[c], i), pair(xs.at[1 - c], i)], 0)
+        xs_turned[i] = jnp.transpose(rows_i.astype(F32)).astype(BF16)
+        return carry
+
+    lax.fori_loop(0, Y, turn, 0)
     for copy in x_swaps:
         copy.wait_recv()
 
@@ -512,26 +531,23 @@
     dpre_own[1] = pre_grad[:, C:]
     dpre_swap = go(remote(dpre_own.at[1 - c], dpre_other, s_send.at[3], s_recv.at[4], sibling))
 
-    hid_swap.wait_recv()
     whole = gr.at[1 - c]
     pltpu.make_async_copy(whole, whole, s_recv.at[3]).wait()
-    hidden_all = cat([hid_own[c], hid_other[...]], 0)
 
     def back_second(i, carry):
         a, b = span(i)
-        out = dot(hidden_all, cat([pair(gr.at[c], i), pair(gr.at[1 - c], i)], 0), 0, 0).astype(BF16)
+        out = dot(hid_turned[...], cat([pair(gr.at[c], i), pair(gr.at[1 - c], i)], 0)).astype(BF16)
         g2_ref[:, a] = out[:, :C]
         g2_ref[:, b] = out[:, C:]
         return carry
 
     lax.fori_loop(0, Y, back_second, 0)
-    xs_swap.wait_recv()
     dpre_swap.wait_recv()
     pre_grad_all = cat([dpre_own[c], dpre_other[...]], 0)
 
     def back_first(i, carry):
         a, b = span(i)
-        out = dot(cat([pair(xs.at[c], i), pair(xs.at[1 - c], i)], 0), pre_grad_all, 0, 0).astype(BF16)
+        out = dot(xs_turned[i], pre_grad_all).astype(BF16)
         g1_ref[a] = out[:C]
         g1_ref[b] = out[C:]
         return carry
@@ -596,6 +612,8 @@
             vmem((R, hid), BF16),
             vmem((2, R, hid), BF16),
             vmem((R, hid), BF16),
+            vmem((hid, 2 * R), BF16),
+            vmem((Y, X * C, 2 * R), BF16),
             dma((10,)),
             dma((4,)),
             dma((4,)),

time: 116 us -> 111 us (0.957)
  Pallas kernels: 112 us -> 107 us
    pallas_call x1, Pallas kernels: 112 us -> 107 us  [on_device(): pl.pallas_call(functools.partial(kernel, experts, Y), out_shape=(jax.Shap...]
where the time goes in v3:
time: 111 us; the launch traced here: 110 us
  Pallas kernels  107 us (96%)
  local copies, waits for them, and re-layouts  2.72 us (2%)
    pallas_call x1, Pallas kernels, on_device(): pl.pallas_call(functools.partial(kernel, experts, Y), out_shape=(jax.Shap...  107 us
    unnamed x4, local copies, waits for them, and re-layouts  2.72 us

profile of v3, /device:TPU:1, one launch (start us, length us, event | category | flops | bytes accessed | tf_op | source)
XLA Modules:
  0.0 110.5 jit_solution(8844525461424620802)
XLA Ops:
  0.6 107.1 %shard_map.95 = (bf16[2048,128]{1,0:T(8,128)(2,1)}, bf16[128,2048]{1,0:T(8,128)(2,1)}) custom-call(bf16[128,2048]{1,0:T(8,128)(2,1)} %xt_hbm.1, bf16[128,2048]{1,0:T(8,128)(2,1)} %xs_hbm.1, s32[1,128]{1,0:T(1,128)} %bitcast.14, s32[1,128]{1,0:T(1,128)} %bitcast.15, bf16[2048,128]{1,0:T(8,128)(2,1)} %bitcast.10, bf16[128,2048]{1,0:T(8,128)(2,1)} %bitcast.11, ...), custom_call_target="tpu_custom_call" | custom-call | tf_op jit(solution)/shard_map/pallas_call | solution.py:576
  107.8 0.0 copy-start
  107.8 1.9 %copy.12 = bf16[1,2048,128]{2,1,0:T(8,128)(2,1)} copy(bf16[1,2048,128]{2,1,0:T(8,128)(2,1)} %bitcast.9) | data formatting | bytes 1048576
  109.7 0.0 copy-done
  109.7 0.8 copy.13
Async XLA Ops:
  107.8 1.9 %copy-start = (bf16[128,2048]{1,0:T(8,128)(2,1)S(1)}, bf16[128,2048]{1,0:T(8,128)(2,1)}, u32[]{:S(2)}) copy-start(bf16[128,2048]{1,0:T(8,128)(2,1)} %get-tuple-element.5) | copy-start | bytes 1572868
